TPU v7x, 32 devices: a whole 2x2x4 slice. The times are simulated.
32 devices in a mesh: groups: 2 (over x), scene: 16 (over z, y, core).
Axes of the slice: x: 2, y: 2, z: 4, core: 2. Of those that a mesh axis runs over, the one named last changes fastest.
Arguments:
- tokens: bfloat16 [32, 196, 768], P(('groups', 'scene')), parts along dimension 0, may hold values from -6 to 6
- qkv_weight: bfloat16 [768, 2304], replicated, may hold values from -0.21875 to 0.21875
- out_weight: bfloat16 [768, 768], replicated, may hold values from -0.21875 to 0.21875
- attn_gain: float32 [768], replicated, may hold values from 0.1 to 1.9
- head_gain: float32 [768], replicated, may hold values from 0.1 to 1.9
- head_weight: bfloat16 [768, 1024], replicated, may hold values from -0.21875 to 0.21875
- head_bias: float32 [1024], replicated, may hold values from -3 to 3
- pair_list: int32 [64, 2], P('groups'), parts along dimension 0, may hold values from 0 to 15, as said below
- pair_count: int32 [32], P('groups'), parts along dimension 0, may hold values from 1 to 2, as said below
Outputs:
- joined: float32 [32, 196, 768], P(('groups', 'scene')), parts along dimension 0
There are 2 independent parts, one for each index of `groups`. A program takes and returns all parts, laid end to end along the dimension named above; an argument that names none is the same for every part. Nothing has to cross between parts.
Inputs may be any that keep to these rules, and one draw needn't show every extreme that they name: `pair_list`: slot j of device d (row d * 2 + j) holds a pair whose first image is d + (j mod 1); its second image is owned by a device 1 to 2 places away along the scene axis taken as a cycle, image i being owned by device i. `pair_count`: entry d is the number of live slots of device d; slots from that number on are ignored. In every draw some device has exactly 2 and another exactly 1.
All inputs are finite; a program needn't handle non-finite values.
Results may differ from a plain program's by a relative error of at most 0.0045.
Values may be sent and summed in bfloat16 or wider, within the bound.
A program may use at most 128 MiB of HBM per device.

v0:
```python
import jax
import jax.numpy as jnp
from jax import lax
from jax.sharding import PartitionSpec as P

HEADS = 12
REACH = 2


TEMPER = 16.0
CONF_RANGE = 4.0
EPSILON = 1e-06


def shifted(value, axis, steps):
    count = lax.axis_size(axis)
    pairs = [(source, (source + steps) % count) for source in range(count)]
    return lax.ppermute(value, axis, pairs)


def layer_norm(values, gain_vec):
    centred = values - jnp.mean(values, axis=-1, keepdims=True)
    spread = jnp.mean(centred * centred, axis=-1, keepdims=True)
    return centred * lax.rsqrt(spread + EPSILON) * gain_vec


def head_unit(values):
    shaped = values.reshape(values.shape[:-1] + (HEADS, values.shape[-1] // HEADS))
    energy = jnp.mean(shaped * shaped, axis=-1, keepdims=True)
    return (shaped * lax.rsqrt(energy + EPSILON)).reshape(values.shape)


def normed_rows(token_rows, attn_gain):
    return layer_norm(token_rows.astype(jnp.float32), attn_gain).astype(jnp.bfloat16)


def queries_of(normed, weight_cols):
    mixed = jnp.einsum("vtd,de->vte", normed, weight_cols, preferred_element_type=jnp.float32)
    return head_unit(mixed).astype(jnp.bfloat16)


def keys_values_of(normed, weight_cols):
    model_width = normed.shape[-1]
    mixed = jnp.einsum("vtd,de->vte", normed, weight_cols, preferred_element_type=jnp.float32)
    return (
        head_unit(mixed[..., :model_width]).astype(jnp.bfloat16),
        mixed[..., model_width:].astype(jnp.bfloat16),
    )


def view_maps(own_rows, queries, key_rows, values, out_weight, head_gain, head_weight, head_bias):
    view_count, token_count, model_width = own_rows.shape
    head_size = model_width // HEADS
    query_heads = queries.reshape(view_count, token_count, HEADS, head_size)
    key_heads = key_rows.reshape(view_count, token_count, HEADS, head_size)
    value_heads = values.reshape(view_count, token_count, HEADS, head_size)
    scores = jnp.einsum(
        "vthc,vshc->vhts", query_heads, key_heads, preferred_element_type=jnp.float32
    ) * (TEMPER / head_size)
    exponent = jnp.exp(scores)
    attention = (exponent / jnp.sum(exponent, axis=-1, keepdims=True)).astype(jnp.bfloat16)
    attended = jnp.einsum(
        "vhts,vshc->vthc", attention, value_heads, preferred_element_type=jnp.float32
    )
    attended = attended.reshape(view_count, token_count, model_width).astype(jnp.bfloat16)
    mixed = own_rows.astype(jnp.float32) + jnp.einsum(
        "vtd,de->vte", attended, out_weight, preferred_element_type=jnp.float32
    )
    head_in = layer_norm(mixed, head_gain).astype(jnp.bfloat16)
    head_out = (
        jnp.einsum("vtd,de->vte", head_in, head_weight, preferred_element_type=jnp.float32)
        + head_bias
    )
    xyz_cols = 3 * (head_weight.shape[1] // 4)
    return (
        head_out[..., :xyz_cols].astype(jnp.bfloat16),
        head_out[..., xyz_cols:].astype(jnp.bfloat16),
    )


def contributions(xyz, conf, image_ids, live_mask, first_id, span_count):
    view_count, token_count, xyz_cols = xyz.shape
    pixels = conf.shape[-1]
    local_ids = image_ids - first_id
    onehot = (local_ids[None, :] == jnp.arange(span_count, dtype=jnp.int32)[:, None]).astype(
        jnp.float32
    ) * live_mask[None, :]
    weight = jnp.exp(CONF_RANGE * jnp.tanh(conf.astype(jnp.float32) / CONF_RANGE))
    weighted = (
        weight[:, :, None, :] * xyz.astype(jnp.float32).reshape(view_count, token_count, 3, pixels)
    ).reshape(view_count, token_count, xyz_cols)
    weighted_sum = jnp.einsum("iv,vtx->itx", onehot, weighted, precision=lax.Precision.HIGHEST)
    weight_sum = jnp.einsum("iv,vtp->itp", onehot, weight, precision=lax.Precision.HIGHEST)
    return (weighted_sum, weight_sum)


def per_device(
    tokens,
    qkv_weight,
    out_weight,
    attn_gain,
    head_gain,
    head_weight,
    head_bias,
    pair_list,
    pair_count,
):
    image_count, token_count, model_width = tokens.shape
    scene_size = lax.axis_size("scene")
    position = lax.axis_index("scene")
    pair_slots = pair_list.shape[0] // scene_size
    my_pairs = lax.dynamic_slice_in_dim(pair_list, position * pair_slots, pair_slots, 0)
    own_ids = jnp.concatenate([my_pairs[:, 0], my_pairs[:, 1]])
    partner_ids = jnp.concatenate([my_pairs[:, 1], my_pairs[:, 0]])
    cycle_images = scene_size * image_count
    window_start = (position - REACH) * image_count
    own_local = (own_ids - window_start) % cycle_images
    partner_local = (partner_ids - window_start) % cycle_images
    blocks = []
    for offset in range(-REACH, REACH + 1):
        if offset == 0:
            blocks.append(tokens)
        else:
            blocks.append(shifted(tokens, "scene", -offset))
    window = jnp.concatenate(blocks, axis=0)
    own_rows = window[own_local]
    partner_rows = window[partner_local]
    queries = queries_of(normed_rows(own_rows, attn_gain), qkv_weight[:, :model_width])
    key_rows, values = keys_values_of(
        normed_rows(partner_rows, attn_gain), qkv_weight[:, model_width:]
    )
    xyz, conf = view_maps(
        own_rows, queries, key_rows, values, out_weight, head_gain, head_weight, head_bias
    )
    slot_live = (jnp.arange(pair_slots, dtype=jnp.int32) < pair_count[position]).astype(jnp.float32)
    live_mask = jnp.concatenate([slot_live, slot_live])
    window_sum, window_weight = contributions(
        xyz, conf, own_local, live_mask, 0, (2 * REACH + 1) * image_count
    )
    middle = REACH * image_count
    weighted_sum = window_sum[middle : middle + image_count]
    weight_sum = window_weight[middle : middle + image_count]
    for offset in range(-REACH, REACH + 1):
        if offset != 0:
            row_start = (offset + REACH) * image_count
            arrived_sum, arrived_weight = (
                shifted(
                    window_sum[row_start : row_start + image_count].astype(jnp.bfloat16),
                    "scene",
                    offset,
                ).astype(jnp.float32),
                shifted(
                    window_weight[row_start : row_start + image_count].astype(jnp.bfloat16),
                    "scene",
                    offset,
                ).astype(jnp.float32),
            )
            weighted_sum = weighted_sum + arrived_sum
            weight_sum = weight_sum + arrived_weight
    return weighted_sum / jnp.tile(weight_sum, (1, 1, 3))


def solution(mesh):
    return jax.shard_map(
        per_device,
        mesh=mesh,
        in_specs=(
            P(("groups", "scene"), None, None),
            P(),
            P(),
            P(),
            P(),
            P(),
            P(),
            P("groups", None),
            P("groups"),
        ),
        out_specs=P(("groups", "scene"), None, None),
        check_vma=False,
    )
```

profile of v0, /device:TPU:0, one launch (start us, length us, event | category | flops | bytes accessed | tf_op | source)
XLA Modules:
  0.0 148.5 jit_solution(17032723547600941379)
XLA Ops:
  0.0 5.4 %collective-permute-start.2 = (bf16[1,196,768]{2,1,0:T(8,128)(2,1)}, bf16[1,196,768]{2,1,0:T(8,128)(2,1)S(1)}, u32[]{:S(2)}, u32[]{:S(2)}) collective-permute-start(bf16[1,196,768]{2,1,0:T(8,128)(2,1)} %param.9), channel_id=1, source_target_pairs={{0,15},{1,0},{2,1},{3,2},{4,3},{5,4},{6,5},{7,6},{8,7},{9,8},{10,9... | collective-permute-start | bytes 903176 | tf_op jit(solution)/shard_map/ppermute | solution.py:18
  5.5 4.8 %collective-permute-start.3 = (bf16[1,196,768]{2,1,0:T(8,128)(2,1)}, bf16[1,196,768]{2,1,0:T(8,128)(2,1)S(1)}, u32[]{:S(2)}, u32[]{:S(2)}) collective-permute-start(bf16[1,196,768]{2,1,0:T(8,128)(2,1)} %param.9), channel_id=1, source_target_pairs={{0,14},{1,15},{2,0},{3,1},{4,2},{5,3},{6,4},{7,5},{8,6},{9,7},{10,... | collective-permute-start | bytes 903176 | tf_op jit(solution)/shard_map/ppermute | solution.py:18
  10.2 1.2 dynamic_slice.7
  11.4 0.6 iota_compare_fusion.3
  12.1 0.8 constant_dynamic-slice_fusion
  12.9 0.1 fusion.56
  13.0 0.1 add_convert_fusion.1
  13.0 0.1 and_select_fusion.2
  13.1 8.2 %collective-permute-done = bf16[1,196,768]{2,1,0:T(8,128)(2,1)S(1)} collective-permute-done((bf16[1,196,768]{2,1,0:T(8,128)(2,1)}, bf16[1,196,768]{2,1,0:T(8,128)(2,1)S(1)}, u32[]{:S(2)}, u32[]{:S(2)}) %collective-permute-start) | collective-permute-done | bytes 301088 | tf_op jit(solution)/shard_map/ppermute | solution.py:18
  21.4 1.0 constant_dynamic-update-slice_fusion.2
  22.4 2.0 %collective-permute-done.3 = bf16[1,196,768]{2,1,0:T(8,128)(2,1)S(1)} collective-permute-done((bf16[1,196,768]{2,1,0:T(8,128)(2,1)}, bf16[1,196,768]{2,1,0:T(8,128)(2,1)S(1)}, u32[]{:S(2)}, u32[]{:S(2)}) %collective-permute-start.3) | collective-permute-done | bytes 301088 | tf_op jit(solution)/shard_map/ppermute | solution.py:18
  24.5 1.2 copy-done.2
  25.7 2.0 %gather_fusion.1 = bf16[4,196,768]{2,1,0:T(8,128)(2,1)S(1)} fusion(bf16[5,196,768]{2,1,0:T(8,128)(2,1)} %copy-done.2, s32[1024]{0:T(1024)S(1)} %get-tuple-element.29), kind=kCustom, calls=%fused_computation.1 | custom fusion | bytes 2408464 | tf_op jit(solution)/shard_map/gather | solution.py:127
  27.7 0.2 convert_reduce_fusion.1
  28.0 0.5 fusion.9
  28.5 4.0 %fusion.14 = f32[4,196,1536]{2,1,0:T(8,128)S(1)} fusion(bf16[768,2304]{1,0:T(8,128)(2,1)} %param.10, bf16[4,196,768]{2,1,0:T(8,128)(2,1)S(1)} %gather_fusion.1, f32[768]{0:T(1024)S(1)} %copy-done.5, f32[4,196]{1,0:T(4,128)S(1)} %add_rsqrt_fusion.4, f32[4,196]{1,0:T(4,128)S(1)} %broadcast_multiply_fusion.2), kind=kOutput, calls=%fused_computation.30 | convolution fusion | flops 1852698624 | bytes 8389760 | tf_op jit(solution)/shard_map/vtd,de->vte/dot_general | solution.py:44
  32.5 1.3 slice.132
  33.8 2.1 %slice_multiply_fusion = f32[4,196,768]{2,1,0:T(8,128)} fusion(f32[4,196,1536]{2,1,0:T(8,128)S(1)} %fusion.14), kind=kLoop, calls=%fused_computation.33 | loop fusion | flops 602112 | bytes 4816896 | tf_op jit(solution)/shard_map/mul | solution.py:29
  35.9 2.0 %gather_fusion = bf16[4,196,768]{2,1,0:T(8,128)(2,1)S(1)} fusion(bf16[5,196,768]{2,1,0:T(8,128)(2,1)} %copy-done.2, s32[1024]{0:T(1024)S(1)} %get-tuple-element.30), kind=kCustom, calls=%fused_computation | custom fusion | bytes 2408464 | tf_op jit(solution)/shard_map/gather | solution.py:126
  37.9 0.2 convert_reduce_fusion
  38.2 0.5 fusion.6
  38.7 2.5 %copy.29 = bf16[4,196,768]{1,2,0:T(8,128)(2,1)} copy(bf16[4,196,768]{2,1,0:T(8,128)(2,1)} %slice.132) | data formatting | bytes 2408448 | tf_op jit(solution)/shard_map/slice | solution.py:47
  41.2 3.4 %copy.33 = f32[4,196,768]{1,2,0:T(8,128)} copy(f32[4,196,768]{2,1,0:T(8,128)} %slice_multiply_fusion) | data formatting | bytes 4816896 | tf_op jit(solution)/shard_map/mul | solution.py:29
  44.6 2.3 %reduce_sum.86 = f32[4,196,12]{1,2,0:T(8,128)S(1)} reduce(f32[4,196,12,64]{1,3,2,0:T(8,128)} %bitcast.54, f32[]{:T(128)} %constant.52.clone.1), dimensions={3}, to_apply=%region_5.6 | reduce | flops 592704 | bytes 2446084 | tf_op jit(solution)/shard_map/reduce_sum | solution.py:29
  46.9 1.9 %mul.139 = f32[4,196,12,64]{1,3,2,0:T(8,128)} broadcast(f32[4,196,12]{1,2,0:T(8,128)S(1)} %add_rsqrt_fusion), dimensions={0,1,2} | broadcast | bytes 2446080 | tf_op jit(solution)/shard_map/mul | solution.py:30
  48.8 3.4 %copy.34 = f32[4,196,768]{2,1,0:T(8,128)} copy(f32[4,196,768]{1,2,0:T(8,128)} %bitcast.51) | data formatting | bytes 4816896 | tf_op jit(solution)/shard_map/mul | solution.py:30
  52.1 3.7 %multiply_convert_fusion.1 = bf16[4,196,768]{2,1,0:T(8,128)(2,1)} fusion(f32[4,196,768]{2,1,0:T(8,128)} %copy.34, f32[4,196,1536]{2,1,0:T(8,128)} %copy-done.1), kind=kLoop, calls=%fused_computation.26 | loop fusion | flops 1204224 | bytes 6021120 | tf_op jit(solution)/shard_map/convert_element_type | solution.py:46
  55.9 2.6 %copy.35 = bf16[4,196,768]{1,2,0:T(8,128)(2,1)} copy(bf16[4,196,768]{2,1,0:T(8,128)(2,1)} %multiply_convert_fusion.1) | data formatting | bytes 2408448 | tf_op jit(solution)/shard_map/convert_element_type | solution.py:46
  58.4 4.8 %fusion.62 = (f32[4,196,768]{2,1,0:T(8,128)}, f32[4,196,768]{2,1,0:T(8,128)}) fusion(bf16[768,2304]{1,0:T(8,128)(2,1)} %param.10, bf16[4,196,768]{2,1,0:T(8,128)(2,1)S(1)} %gather_fusion, f32[4,196]{1,0:T(4,128)S(1)} %add_rsqrt_fusion.3, f32[4,196]{1,0:T(4,128)S(1)} %broadcast_multiply_fusion.1, f32[768]{0:T(1024)S(1)} %copy-done.5), kind=kOutput, calls=%fused_computation.121 | convolution fusion | flops 928456704 | bytes 7210112 | tf_op jit(solution)/shard_map/vtd,de->vte/dot_general | solution.py:38
  63.2 3.4 %copy.30 = f32[4,196,768]{1,2,0:T(8,128)} copy(f32[4,196,768]{2,1,0:T(8,128)} %get-tuple-element.19) | data formatting | bytes 4816896 | tf_op jit(solution)/shard_map/mul | solution.py:29
  66.6 2.3 %reduce_sum.85 = f32[4,196,12]{1,2,0:T(8,128)S(1)} reduce(f32[4,196,12,64]{1,3,2,0:T(8,128)} %bitcast.53, f32[]{:T(128)} %constant.52.clone.1), dimensions={3}, to_apply=%region_4.5 | reduce | flops 592704 | bytes 2446084 | tf_op jit(solution)/shard_map/reduce_sum | solution.py:29
  68.9 1.9 %mul.134 = f32[4,196,12,64]{1,3,2,0:T(8,128)} broadcast(f32[4,196,12]{1,2,0:T(8,128)S(1)} %add_rsqrt_fusion.1), dimensions={0,1,2} | broadcast | bytes 2446080 | tf_op jit(solution)/shard_map/mul | solution.py:30
  70.8 3.4 %copy.31 = f32[4,196,768]{2,1,0:T(8,128)} copy(f32[4,196,768]{1,2,0:T(8,128)} %bitcast.52) | data formatting | bytes 4816896 | tf_op jit(solution)/shard_map/mul | solution.py:30
  74.2 3.7 %multiply_convert_fusion.2 = bf16[4,196,768]{2,1,0:T(8,128)(2,1)} fusion(f32[4,196,768]{2,1,0:T(8,128)} %get-tuple-element.20, f32[4,196,768]{2,1,0:T(8,128)} %copy.31), kind=kLoop, calls=%fused_computation.27 | loop fusion | flops 1204224 | bytes 6021120 | tf_op jit(solution)/shard_map/convert_element_type | solution.py:39
  77.9 2.5 %copy.32 = bf16[4,196,768]{1,2,0:T(8,128)(2,1)} copy(bf16[4,196,768]{2,1,0:T(8,128)(2,1)} %multiply_convert_fusion.2) | data formatting | bytes 2408448 | tf_op jit(solution)/shard_map/convert_element_type | solution.py:39
  80.5 4.2 %fusion = (f32[4,12,196]{2,1,0:T(8,128)S(1)}, f32[4,12,196,196]{2,3,1,0:T(8,128)S(1)}) fusion(bf16[4,196,12,64]{1,3,2,0:T(8,128)(2,1)} %bitcast.56, bf16[4,196,12,64]{1,3,2,0:T(8,128)(2,1)} %bitcast.55), kind=kOutput, calls=%fused_computation.4 | convolution fusion | flops 239706432 | bytes 9821952 | tf_op jit(solution)/shard_map/vthc,vshc->vhts/dot_general | solution.py:57
  84.6 2.3 %fusion.17 = bf16[4,12,64,196]{3,2,1,0:T(8,128)(2,1)S(1)} fusion(bf16[4,196,12,64]{1,3,2,0:T(8,128)(2,1)S(1)} %bitcast.57, f32[4,12,196,196]{2,3,1,0:T(8,128)S(1)} %get-tuple-element.22, f32[4,12,196]{2,1,0:T(8,128)S(1)} %get-tuple-element.21), kind=kOutput, calls=%fused_computation.34 | convolution fusion | flops 242161920 | bytes 9821952 | tf_op jit(solution)/shard_map/vhts,vshc->vthc/dot_general | solution.py:62
  87.0 1.4 fusion.63
  88.4 0.4 multiply_reduce_fusion
  88.8 0.2 copy-done.7
  89.1 1.6 %add_convert_fusion = bf16[4,196,1024]{2,1,0:T(8,128)(2,1)S(1)} fusion(f32[1024]{0:T(1024)S(1)} %copy-done.7, bf16[768,1024]{1,0:T(8,128)(2,1)S(1)} %copy-done, f32[4,196,768]{2,1,0:T(8,128)S(1)} %get-tuple-element.24, f32[768]{0:T(1024)S(1)} %copy-done.8, f32[4,196]{1,0:T(4,128)S(1)} %add_rsqrt_fusion.2, f32[4,196]{1,0:T(4,128)S(1)} %broadcast_multiply_fusion), kind=kOutput, calls=%fused_computation.9 | convolution fusion | flops 1237139456 | bytes 5600384 | tf_op jit(solution)/shard_map/vtd,de->vte/dot_general | solution.py:71
  90.7 0.2 multiply_exponential_fusion.1
  90.9 2.0 %fusion.65 = (bf16[5,196,256]{2,0,1:T(8,128)(2,1)S(1)}, f32[5,196,256]{2,0,1:T(8,128)S(1)}) fusion(f32[4,196,256]{2,1,0:T(8,128)S(1)} %multiply_exponential_fusion.1, f32[4]{0:T(128)S(1)} %add_convert_fusion.1, s32[4]{0:T(128)S(1)} %and_select_fusion.2), kind=kOutput, calls=%fused_computation.124 | convolution fusion | flops 12293160 | bytes 2308128 | tf_op jit(solution)/shard_map/iv,vtp->itp/dot_general | solution.py:93
  92.9 1.5 fusion.61
  94.4 3.4 %collective-permute-start.8 = (bf16[1,196,256]{2,0,1:T(2,128)(2,1)}, bf16[1,196,256]{2,0,1:T(2,128)(2,1)}, u32[]{:S(2)}, u32[]{:S(2)}) collective-permute-start(bf16[1,196,256]{2,0,1:T(2,128)(2,1)} %get-tuple-element.9), channel_id=1, source_target_pairs={{0,14},{1,15},{2,0},{3,1},{4,2},{5,3},{6,4},{7,5},{8,6},{9,7},{10,... | collective-permute-start | bytes 301064 | tf_op jit(solution)/shard_map/ppermute | solution.py:18
  97.8 1.8 %collective-permute-start.10 = (bf16[1,196,256]{2,0,1:T(2,128)(2,1)}, bf16[1,196,256]{2,0,1:T(2,128)(2,1)}, u32[]{:S(2)}, u32[]{:S(2)}) collective-permute-start(bf16[1,196,256]{2,0,1:T(2,128)(2,1)} %get-tuple-element.11), channel_id=1, source_target_pairs={{0,1},{1,2},{2,3},{3,4},{4,5},{5,6},{6,7},{7,8},{8,9},{9,10},{10,1... | collective-permute-start | bytes 301064 | tf_op jit(solution)/shard_map/ppermute | solution.py:18
  99.6 4.0 %collective-permute-start.9 = (bf16[1,196,256]{2,0,1:T(2,128)(2,1)}, bf16[1,196,256]{2,0,1:T(2,128)(2,1)}, u32[]{:S(2)}, u32[]{:S(2)}) collective-permute-start(bf16[1,196,256]{2,0,1:T(2,128)(2,1)} %get-tuple-element.12), channel_id=1, source_target_pairs={{0,15},{1,0},{2,1},{3,2},{4,3},{5,4},{6,5},{7,6},{8,7},{9,8},{10,9... | collective-permute-start | bytes 301064 | tf_op jit(solution)/shard_map/ppermute | solution.py:18
  103.7 2.2 %mul.150 = f32[4,196,3,256]{3,2,1,0:T(4,128)} broadcast(f32[4,196,256]{2,1,0:T(8,128)S(1)} %multiply_exponential_fusion.1), dimensions={0,1,3} | broadcast | bytes 3211264 | tf_op jit(solution)/shard_map/mul | solution.py:90
  105.9 4.8 %mul.151 = f32[4,196,768]{2,1,0:T(8,128)} reshape(f32[4,196,3,256]{3,2,1,0:T(4,128)} %mul.150) | data formatting | bytes 4816896 | tf_op jit(solution)/shard_map/mul | solution.py:90
  110.7 2.3 %convert_multiply_fusion = f32[4,196,768]{2,1,0:T(8,128)S(1)} fusion(f32[4,196,768]{2,1,0:T(8,128)} %mul.151, bf16[4,196,1024]{2,1,0:T(8,128)(2,1)} %copy-done.3), kind=kLoop, calls=%fused_computation.23 | loop fusion | flops 1204224 | bytes 6021120 | tf_op jit(solution)/shard_map/mul | solution.py:90
  113.0 7.0 %fusion.64 = (bf16[5,196,768]{2,0,1:T(8,128)(2,1)S(1)}, f32[5,196,768]{2,0,1:T(8,128)}) fusion(f32[4,196,768]{2,1,0:T(8,128)S(1)} %convert_multiply_fusion, f32[4]{0:T(128)S(1)} %add_convert_fusion.1, s32[4]{0:T(128)S(1)} %and_select_fusion.2), kind=kOutput, calls=%fused_computation.123 | convolution fusion | flops 36879400 | bytes 6924320 | tf_op jit(solution)/shard_map/iv,vtx->itx/dot_general | solution.py:92
  120.0 1.8 %fusion.60 = (bf16[1,196,768]{2,0,1:T(2,128)(2,1)S(1)}, bf16[1,196,768]{2,0,1:T(2,128)(2,1)S(1)}, bf16[1,196,768]{2,0,1:T(2,128)(2,1)S(1)}, bf16[1,196,768]{2,0,1:T(2,128)(2,1)S(1)}) fusion(bf16[5,196,768]{2,0,1:T(8,128)(2,1)S(1)} %get-tuple-element.25), kind=kLoop, calls=%fused_computation.119 | loop fusion | bytes 2408448 | tf_op jit(solution)/shard_map/slice | solution.py:148
  121.8 0.8 copy.45
  122.5 0.8 copy.43
  123.3 0.8 copy.41
  124.1 0.5 collective-permute-start.5
  124.7 4.7 %collective-permute-start.4 = (bf16[1,196,768]{2,1,0:T(8,128)(2,1)S(1)}, bf16[1,196,768]{2,1,0:T(8,128)(2,1)}, u32[]{:S(2)}, u32[]{:S(2)}) collective-permute-start(bf16[1,196,768]{2,1,0:T(8,128)(2,1)S(1)} %copy.39), channel_id=1, source_target_pairs={{0,14},{1,15},{2,0},{3,1},{4,2},{5,3},{6,4},{7,5},{8,6},{9,7},{10,... | collective-permute-start | bytes 903176 | tf_op jit(solution)/shard_map/ppermute | solution.py:18
  129.4 1.9 %convert_add_fusion.1 = f32[1,196,256]{2,0,1:T(1,128)S(1)} fusion(bf16[1,196,256]{2,0,1:T(2,128)(2,1)} %collective-permute-done.11, bf16[1,196,256]{2,0,1:T(2,128)(2,1)} %collective-permute-done.10, bf16[1,196,256]{2,0,1:T(2,128)(2,1)} %collective-permute-done.9, bf16[1,196,256]{2,0,1:T(2,128)(2,1)} %collective-permute-done.8, ...), kind=kLoop, calls=%fused_computation.65 | loop fusion | flops 401408 | bytes 802816 | tf_op jit(solution)/shard_map/add | solution.py:159
  131.3 0.1 tile.12
  131.4 0.8 tile.14
  132.3 4.4 %collective-permute-done.6 = bf16[1,196,768]{2,1,0:T(8,128)(2,1)} collective-permute-done((bf16[1,196,768]{2,1,0:T(8,128)(2,1)}, bf16[1,196,768]{2,1,0:T(8,128)(2,1)}, u32[]{:S(2)}, u32[]{:S(2)}) %collective-permute-start.6) | collective-permute-done | bytes 301088 | tf_op jit(solution)/shard_map/ppermute | solution.py:18
  136.7 1.9 %collective-permute-done.7 = bf16[1,196,768]{2,1,0:T(8,128)(2,1)} collective-permute-done((bf16[1,196,768]{2,1,0:T(8,128)(2,1)}, bf16[1,196,768]{2,1,0:T(8,128)(2,1)}, u32[]{:S(2)}, u32[]{:S(2)}) %collective-permute-start.7) | collective-permute-done | bytes 301088 | tf_op jit(solution)/shard_map/ppermute | solution.py:18
  138.6 5.5 %collective-permute-done.4 = bf16[1,196,768]{2,1,0:T(8,128)(2,1)} collective-permute-done((bf16[1,196,768]{2,1,0:T(8,128)(2,1)S(1)}, bf16[1,196,768]{2,1,0:T(8,128)(2,1)}, u32[]{:S(2)}, u32[]{:S(2)}) %collective-permute-start.4) | collective-permute-done | bytes 301088 | tf_op jit(solution)/shard_map/ppermute | solution.py:18
  144.1 4.4 %fusion.39 = f32[1,196,768]{2,0,1:T(1,128)} fusion(f32[1,196,768]{2,0,1:T(1,128)S(1)} %tile.14, bf16[1,196,768]{2,1,0:T(8,128)(2,1)} %collective-permute-done.7, bf16[1,196,768]{2,1,0:T(8,128)(2,1)} %collective-permute-done.6, bf16[1,196,768]{2,1,0:T(8,128)(2,1)} %collective-permute-done.5, bf16[1,196,768]{2,1,0:T(8,128)(2,1)} %collective-permute-done.4, ...), kind=kLoop, calls=%fused_computation.57 | loop fusion | flops 1354752 | bytes 3010560 | tf_op jit(solution)/shard_map/div | solution.py:160
  (44 shorter events, 0.4 us)
Async XLA Ops:
  0.0 88.8 %copy-start = (bf16[768,1024]{1,0:T(8,128)(2,1)S(1)}, bf16[768,1024]{1,0:T(8,128)(2,1)}, u32[]{:S(2)}) copy-start(bf16[768,1024]{1,0:T(8,128)(2,1)} %param.14) | copy-start | bytes 4718596
  0.0 22.4 %collective-permute-start.2 = (bf16[1,196,768]{2,1,0:T(8,128)(2,1)}, bf16[1,196,768]{2,1,0:T(8,128)(2,1)S(1)}, u32[]{:S(2)}, u32[]{:S(2)}) collective-permute-start(bf16[1,196,768]{2,1,0:T(8,128)(2,1)} %param.9), channel_id=1, source_target_pairs={{0,15},{1,0},{2,1},{3,2},{4,3},{5,4},{6,5},{7,6},{8,7},{9,8},{10,9... | collective-permute-start | bytes 903176 | tf_op jit(solution)/shard_map/ppermute | solution.py:18
  5.4 15.9 %collective-permute-start.1 = (bf16[1,196,768]{2,1,0:T(8,128)(2,1)}, bf16[1,196,768]{2,1,0:T(8,128)(2,1)S(1)}, u32[]{:S(2)}, u32[]{:S(2)}) collective-permute-start(bf16[1,196,768]{2,1,0:T(8,128)(2,1)} %param.9), channel_id=1, source_target_pairs={{0,1},{1,2},{2,3},{3,4},{4,5},{5,6},{6,7},{7,8},{8,9},{9,10},{10,1... | collective-permute-start | bytes 903176 | tf_op jit(solution)/shard_map/ppermute | solution.py:18
  5.5 15.9 %collective-permute-start = (bf16[1,196,768]{2,1,0:T(8,128)(2,1)}, bf16[1,196,768]{2,1,0:T(8,128)(2,1)S(1)}, u32[]{:S(2)}, u32[]{:S(2)}) collective-permute-start(bf16[1,196,768]{2,1,0:T(8,128)(2,1)} %param.9), channel_id=1, source_target_pairs={{0,2},{1,3},{2,4},{3,5},{4,6},{5,7},{6,8},{7,9},{8,10},{9,11},{10,... | collective-permute-start | bytes 903176 | tf_op jit(solution)/shard_map/ppermute | solution.py:18
  5.5 19.0 %collective-permute-start.3 = (bf16[1,196,768]{2,1,0:T(8,128)(2,1)}, bf16[1,196,768]{2,1,0:T(8,128)(2,1)S(1)}, u32[]{:S(2)}, u32[]{:S(2)}) collective-permute-start(bf16[1,196,768]{2,1,0:T(8,128)(2,1)} %param.9), channel_id=1, source_target_pairs={{0,14},{1,15},{2,0},{3,1},{4,2},{5,3},{6,4},{7,5},{8,6},{9,7},{10,... | collective-permute-start | bytes 903176 | tf_op jit(solution)/shard_map/ppermute | solution.py:18
  24.5 1.2 copy-start.2
  25.7 2.8 %copy-start.5 = (f32[768]{0:T(1024)S(1)}, f32[768]{0:T(1024)}, u32[]{:S(2)}) copy-start(f32[768]{0:T(1024)} %param.12) | copy-start | bytes 9220
  32.5 3.4 %copy-start.1 = (f32[4,196,1536]{2,1,0:T(8,128)}, f32[4,196,1536]{2,1,0:T(8,128)S(1)}, u32[]{:S(2)}) copy-start(f32[4,196,1536]{2,1,0:T(8,128)S(1)} %fusion.14) | copy-start | bytes 14450692
  80.4 4.2 %copy-start.4 = (bf16[4,196,768]{1,2,0:T(8,128)(2,1)S(1)}, bf16[4,196,768]{1,2,0:T(8,128)(2,1)}, u32[]{:S(2)}) copy-start(bf16[4,196,768]{1,2,0:T(8,128)(2,1)} %copy.29) | copy-start | bytes 3612676
  84.6 2.4 %copy-start.6 = (bf16[768,768]{1,0:T(8,128)(2,1)S(1)}, bf16[768,768]{1,0:T(8,128)(2,1)}, u32[]{:S(2)}) copy-start(bf16[768,768]{1,0:T(8,128)(2,1)} %param.11) | copy-start | bytes 3538948
  88.3 0.7 copy-start.7
  88.4 0.7 copy-start.8
  90.7 3.7 %copy-start.3 = (bf16[4,196,1024]{2,1,0:T(8,128)(2,1)}, bf16[4,196,1024]{2,1,0:T(8,128)(2,1)S(1)}, u32[]{:S(2)}) copy-start(bf16[4,196,1024]{2,1,0:T(8,128)(2,1)S(1)} %add_convert_fusion) | copy-start | bytes 4816900
  94.4 30.2 %collective-permute-start.8 = (bf16[1,196,256]{2,0,1:T(2,128)(2,1)}, bf16[1,196,256]{2,0,1:T(2,128)(2,1)}, u32[]{:S(2)}, u32[]{:S(2)}) collective-permute-start(bf16[1,196,256]{2,0,1:T(2,128)(2,1)} %get-tuple-element.9), channel_id=1, source_target_pairs={{0,14},{1,15},{2,0},{3,1},{4,2},{5,3},{6,4},{7,5},{8,6},{9,7},{10,... | collective-permute-start | bytes 301064 | tf_op jit(solution)/shard_map/ppermute | solution.py:18
  97.8 26.8 %collective-permute-start.11 = (bf16[1,196,256]{2,0,1:T(2,128)(2,1)}, bf16[1,196,256]{2,0,1:T(2,128)(2,1)}, u32[]{:S(2)}, u32[]{:S(2)}) collective-permute-start(bf16[1,196,256]{2,0,1:T(2,128)(2,1)} %get-tuple-element.10), channel_id=1, source_target_pairs={{0,2},{1,3},{2,4},{3,5},{4,6},{5,7},{6,8},{7,9},{8,10},{9,11},{10,... | collective-permute-start | bytes 301064 | tf_op jit(solution)/shard_map/ppermute | solution.py:18
  97.8 26.9 %collective-permute-start.10 = (bf16[1,196,256]{2,0,1:T(2,128)(2,1)}, bf16[1,196,256]{2,0,1:T(2,128)(2,1)}, u32[]{:S(2)}, u32[]{:S(2)}) collective-permute-start(bf16[1,196,256]{2,0,1:T(2,128)(2,1)} %get-tuple-element.11), channel_id=1, source_target_pairs={{0,1},{1,2},{2,3},{3,4},{4,5},{5,6},{6,7},{7,8},{8,9},{9,10},{10,1... | collective-permute-start | bytes 301064 | tf_op jit(solution)/shard_map/ppermute | solution.py:18
  99.6 29.8 %collective-permute-start.9 = (bf16[1,196,256]{2,0,1:T(2,128)(2,1)}, bf16[1,196,256]{2,0,1:T(2,128)(2,1)}, u32[]{:S(2)}, u32[]{:S(2)}) collective-permute-start(bf16[1,196,256]{2,0,1:T(2,128)(2,1)} %get-tuple-element.12), channel_id=1, source_target_pairs={{0,15},{1,0},{2,1},{3,2},{4,3},{5,4},{6,5},{7,6},{8,7},{9,8},{10,9... | collective-permute-start | bytes 301064 | tf_op jit(solution)/shard_map/ppermute | solution.py:18
  124.1 8.2 %collective-permute-start.5 = (bf16[1,196,768]{2,1,0:T(8,128)(2,1)}, bf16[1,196,768]{2,1,0:T(8,128)(2,1)}, u32[]{:S(2)}, u32[]{:S(2)}) collective-permute-start(bf16[1,196,768]{2,1,0:T(8,128)(2,1)} %copy.41), channel_id=1, source_target_pairs={{0,15},{1,0},{2,1},{3,2},{4,3},{5,4},{6,5},{7,6},{8,7},{9,8},{10,9... | collective-permute-start | bytes 903176 | tf_op jit(solution)/shard_map/ppermute | solution.py:18
  124.6 12.1 %collective-permute-start.6 = (bf16[1,196,768]{2,1,0:T(8,128)(2,1)}, bf16[1,196,768]{2,1,0:T(8,128)(2,1)}, u32[]{:S(2)}, u32[]{:S(2)}) collective-permute-start(bf16[1,196,768]{2,1,0:T(8,128)(2,1)} %copy.43), channel_id=1, source_target_pairs={{0,1},{1,2},{2,3},{3,4},{4,5},{5,6},{6,7},{7,8},{8,9},{9,10},{10,1... | collective-permute-start | bytes 903176 | tf_op jit(solution)/shard_map/ppermute | solution.py:18
  124.6 14.0 %collective-permute-start.7 = (bf16[1,196,768]{2,1,0:T(8,128)(2,1)}, bf16[1,196,768]{2,1,0:T(8,128)(2,1)}, u32[]{:S(2)}, u32[]{:S(2)}) collective-permute-start(bf16[1,196,768]{2,1,0:T(8,128)(2,1)} %copy.45), channel_id=1, source_target_pairs={{0,2},{1,3},{2,4},{3,5},{4,6},{5,7},{6,8},{7,9},{8,10},{9,11},{10,... | collective-permute-start | bytes 903176 | tf_op jit(solution)/shard_map/ppermute | solution.py:18
  124.7 19.4 %collective-permute-start.4 = (bf16[1,196,768]{2,1,0:T(8,128)(2,1)S(1)}, bf16[1,196,768]{2,1,0:T(8,128)(2,1)}, u32[]{:S(2)}, u32[]{:S(2)}) collective-permute-start(bf16[1,196,768]{2,1,0:T(8,128)(2,1)S(1)} %copy.39), channel_id=1, source_target_pairs={{0,14},{1,15},{2,0},{3,1},{4,2},{5,3},{6,4},{7,5},{8,6},{9,7},{10,... | collective-permute-start | bytes 903176 | tf_op jit(solution)/shard_map/ppermute | solution.py:18
where the time goes:
time: 149 us
  local copies, waits for them, and re-layouts  48.4 us (32%)
  matrix products  27.2 us (18%)
  other arithmetic  25.7 us (17%)
  starting transfers between devices  24.7 us (17%)
  waiting for transfers between devices  22.1 us (15%)
    ppermute x12, starting transfers between devices, shifted(): return lax.ppermute(value, axis, pairs)  24.7 us
    ppermute x12, waiting for transfers between devices, shifted(): return lax.ppermute(value, axis, pairs)  22.1 us
    mul x4, local copies, waits for them, and re-layouts, head_unit(): return (shaped * lax.rsqrt(energy + EPSILON)).reshape(values.shape)  10.5 us
    mul x2, local copies, waits for them, and re-layouts, contributions(): weight[:, :, None, :]  7.05 us
    dot_general x1, matrix products, contributions(): jnp.einsum('iv,vtx->itx', onehot, weighted, precision=lax.Precision.HIGHEST)  7.01 us
    mul x2, local copies, waits for them, and re-layouts, head_unit(): energy = jnp.mean(shaped * shaped, axis=-1, keepdims=True)  6.79 us
    dot_general x1, matrix products, queries_of(): jnp.einsum('vtd,de->vte', normed, weight_cols, preferred_element_type=jnp...  4.78 us
    reduce_sum x2, other arithmetic, head_unit(): energy = jnp.mean(shaped * shaped, axis=-1, keepdims=True)  4.55 us
  transfers between devices with their start and end apart: 12, of which 5 were waited for; matrix products, arithmetic and copies ran while one was open for 18% of the time, Pallas kernels for 0%

commit v1 on v0

v1 whole, which is shorter than its diff:
```python
import functools

import jax
import jax.numpy as jnp
from jax import lax
from jax.experimental import pallas as pl
from jax.experimental.pallas import tpu as pltpu
from jax.sharding import PartitionSpec as P

HEADS = 12
TEMPER = 16.0
CONF_RANGE = 4.0
EPSILON = 1e-06
F32 = jnp.float32
BF16 = jnp.bfloat16
MATE, AHEAD, BEHIND, RELAYED = range(4)


def layer_norm(values, gain_row):
    centred = values - jnp.mean(values, axis=-1, keepdims=True)
    spread = jnp.mean(centred * centred, axis=-1, keepdims=True)
    return centred * lax.rsqrt(spread + EPSILON) * gain_row


def product(left, right):
    return jnp.dot(left, right, preferred_element_type=F32)


def scene_kernel(
    n,
    tokens_ref,
    attn_gain_ref,
    head_gain_ref,
    head_bias_ref,
    pairs_ref,
    count_ref,
    qkv_hbm,
    out_hbm,
    head_hbm,
    joined_ref,
    qkv_ref,
    outw_ref,
    headw_ref,
    rows_ref,
    own_ref,
    recv_ref,
    query_ref,
    attended_ref,
    sum_ref,
    weight_ref,
    load_sem,
    send_sem,
    recv_sem,
):
    token_count, width = tokens_ref.shape[1:]
    padded = rows_ref.shape[0]
    head = width // HEADS
    pair = 2 * head
    group = 2 * pair
    pixels = headw_ref.shape[1] // 4
    slots = pairs_ref.shape[1] // n

    me = lax.axis_index("scene")
    sign = 1 - 2 * lax.rem(me, 2)

    def at(steps):
        return lax.rem(me + steps * sign + n, n)

    loads = [
        pltpu.make_async_copy(source, target, load_sem.at[k])
        for k, (source, target) in enumerate(
            ((qkv_hbm, qkv_ref), (out_hbm, outw_ref), (head_hbm, headw_ref))
        )
    ]
    barrier = pltpu.get_barrier_semaphore()
    for steps in (1, 2, -2):
        pl.semaphore_signal(barrier, inc=1, device_id={"scene": at(steps)})
    for load in loads:
        load.start()

    rows_ref[...] = jnp.zeros_like(rows_ref)
    rows_ref[0:token_count] = tokens_ref[0].astype(F32)
    own_ref[...] = layer_norm(rows_ref[...], attn_gain_ref[...]).astype(BF16)
    pl.semaphore_wait(barrier, 3)

    def send(source, slot, steps):
        copy = pltpu.make_async_remote_copy(
            src_ref=source,
            dst_ref=recv_ref.at[slot],
            send_sem=send_sem.at[slot],
            recv_sem=recv_sem.at[slot],
            device_id={"scene": at(steps)},
        )
        copy.start()
        return copy

    copies = {}
    copies[AHEAD] = send(own_ref, AHEAD, -2)
    copies[BEHIND] = send(own_ref, BEHIND, 2)
    copies[MATE] = send(own_ref, MATE, 1)

    across = lax.broadcasted_iota(jnp.int32, (group, group), 0) // head
    along = lax.broadcasted_iota(jnp.int32, (group, group), 1) // head
    same_head = jnp.where(across == along, 1.0 / head, 0.0).astype(BF16)
    first_head = lax.broadcasted_iota(jnp.int32, (padded, pair), 1) < head
    ones = jnp.where(
        lax.broadcasted_iota(jnp.int32, (padded, pair), 0) < token_count, 1.0, 0.0
    ).astype(BF16)

    def unit(mixed):
        energy = product((mixed * mixed).astype(BF16), same_head)
        return mixed * lax.rsqrt(energy + EPSILON)

    loads[0].wait()
    for g in range(width // group):
        queries = unit(product(own_ref[...], qkv_ref[:, g * group : (g + 1) * group]))
        queries = queries * (TEMPER / head)
        for h in range(2):
            block = queries[:, h * pair : (h + 1) * pair]
            query_ref[2 * g + h, 0:padded] = jnp.where(first_head, block, 0.0).astype(BF16)
            query_ref[2 * g + h, padded : 2 * padded] = jnp.where(
                first_head, 0.0, block
            ).astype(BF16)

    def multiplicity(steps):
        other = at(steps)
        total = jnp.float32(0.0)
        for owner, partner in ((me, other), (other, me)):
            for k in range(slots):
                hit = (pairs_ref[1, owner * slots + k] == partner) & (k < count_ref[owner])
                total = total + jnp.where(hit, 1.0, 0.0)
        return total

    def view(slot, steps, first):
        partner = recv_ref[slot]
        for g in range(width // group):
            low = width + g * group
            keys = unit(product(partner, qkv_ref[:, low : low + group])).astype(BF16)
            values = product(
                partner, qkv_ref[:, low + width : low + width + group]
            ).astype(BF16)
            for h in range(2):
                cols = slice(h * pair, (h + 1) * pair)
                scores = lax.dot_general(
                    query_ref[2 * g + h],
                    keys[:, cols],
                    (((1,), (1,)), ((), ())),
                    preferred_element_type=F32,
                )
                mixed = product(
                    jnp.exp(scores).astype(BF16),
                    jnp.concatenate([values[:, cols], ones], axis=1),
                )
                top, bottom = mixed[:padded], mixed[padded:]
                attended_ref[:, g * group + h * pair : g * group + (h + 1) * pair] = (
                    jnp.where(first_head, top[:, :pair], bottom[:, :pair])
                    / jnp.where(first_head, top[:, pair:], bottom[:, pair:])
                ).astype(BF16)
        if first:
            loads[1].wait()
            loads[2].wait()
        mixed = rows_ref[...] + product(attended_ref[...], outw_ref[...])
        head_in = layer_norm(mixed, head_gain_ref[...]).astype(BF16)

        def head_cols(c):
            cols = slice(c * pixels, (c + 1) * pixels)
            made = product(head_in, headw_ref[:, cols]) + head_bias_ref[:, cols]
            return made.astype(BF16).astype(F32)

        weight = jnp.exp(CONF_RANGE * jnp.tanh(head_cols(3) / CONF_RANGE)) * multiplicity(steps)
        weight_ref[...] = weight if first else weight_ref[...] + weight
        for c in range(3):
            cols = slice(c * pixels, (c + 1) * pixels)
            part = weight * head_cols(c)
            sum_ref[:, cols] = part if first else sum_ref[:, cols] + part

    copies[MATE].wait_recv()
    view(MATE, 1, True)
    copies[AHEAD].wait_recv()
    copies[RELAYED] = send(recv_ref.at[AHEAD], RELAYED, 1)
    view(AHEAD, 2, False)
    copies[BEHIND].wait_recv()
    view(BEHIND, -2, False)
    copies[RELAYED].wait_recv()
    view(RELAYED, -1, False)

    for c in range(3):
        cols = slice(c * pixels, (c + 1) * pixels)
        joined_ref[0, :, cols] = (sum_ref[:, cols] / weight_ref[...])[:token_count]
    for slot in range(4):
        copies[slot].wait_send()


def per_device(
    n,
    tokens,
    qkv_weight,
    out_weight,
    attn_gain,
    head_gain,
    head_weight,
    head_bias,
    pair_list,
    pair_count,
):
    _, token_count, width = tokens.shape
    padded = -(-token_count // 16) * 16
    pixels = head_weight.shape[1] // 4
    vmem = pl.BlockSpec(memory_space=pltpu.VMEM)
    smem = pl.BlockSpec(memory_space=pltpu.SMEM)
    hbm = pl.BlockSpec(memory_space=pl.ANY)
    return pl.pallas_call(
        functools.partial(scene_kernel, n),
        out_shape=jax.ShapeDtypeStruct(tokens.shape, F32),
        in_specs=[vmem] * 4 + [smem] * 2 + [hbm] * 3,
        out_specs=vmem,
        scratch_shapes=[
            pltpu.VMEM(qkv_weight.shape, BF16),
            pltpu.VMEM(out_weight.shape, BF16),
            pltpu.VMEM(head_weight.shape, BF16),
            pltpu.VMEM((padded, width), F32),
            pltpu.VMEM((padded, width), BF16),
            pltpu.VMEM((4, padded, width), BF16),
            pltpu.VMEM((HEADS // 2, 2 * padded, 2 * width // HEADS), BF16),
            pltpu.VMEM((padded, width), BF16),
            pltpu.VMEM((padded, 3 * pixels), F32),
            pltpu.VMEM((padded, pixels), F32),
            pltpu.SemaphoreType.DMA((3,)),
            pltpu.SemaphoreType.DMA((4,)),
            pltpu.SemaphoreType.DMA((4,)),
        ],
        compiler_params=pltpu.CompilerParams(
            collective_id=0, has_side_effects=True, vmem_limit_bytes=60 * 2**20
        ),
        name="scene",
    )(
        tokens,
        attn_gain[None],
        head_gain[None],
        head_bias[None],
        pair_list.T,
        pair_count,
        qkv_weight,
        out_weight,
        head_weight,
    )


def solution(mesh):
    return jax.shard_map(
        functools.partial(per_device, mesh.shape["scene"]),
        mesh=mesh,
        in_specs=(
            P(("groups", "scene"), None, None),
            P(),
            P(),
            P(),
            P(),
            P(),
            P(),
            P("groups", None),
            P("groups"),
        ),
        out_specs=P(("groups", "scene"), None, None),
        check_vma=False,
    )
```

time: 149 us -> 35.2 us (0.24)
  local copies, waits for them, and re-layouts: 48.4 us -> 5.04 us
  Pallas kernels: 0 us -> 29.9 us
  matrix products: 27.2 us -> 0 us
  other arithmetic: 25.7 us -> 0 us
  starting transfers between devices: 24.7 us -> 0 us
  waiting for transfers between devices: 22.1 us -> 0 us
    pallas_call x0 -> x1, Pallas kernels: none -> 29.9 us  [per_device(): pl.pallas_call(functools.partial(scene_kernel, n), out_shape=jax.ShapeDty...]
    dot_general x8 -> x0, matrix products: 27.2 us -> none  [the longest x1 7.01 us: contributions(): jnp.einsum('iv,vtx->itx', onehot, weighted, precision=lax.Precision.HIGHEST)]
    ppermute x12 -> x0, starting transfers between devices: 24.7 us -> none  [shifted(): return lax.ppermute(value, axis, pairs)]
    mul x8 -> x0, local copies, waits for them, and re-layouts: 24.4 us -> none  [the longest x4 10.5 us: head_unit(): return (shaped * lax.rsqrt(energy + EPSILON)).reshape(values.shape)]
    ppermute x12 -> x0, waiting for transfers between devices: 22.1 us -> none  [shifted(): return lax.ppermute(value, axis, pairs)]
    slice x8 -> x0, local copies, waits for them, and re-layouts: 9.39 us -> none  [the longest x5 4.07 us: per_device(): window_sum[row_start:row_start + image_count].astype(jnp.bfloat16)]
    convert_element_type x2 -> x0, other arithmetic: 7.42 us -> none  [the longest x1 3.71 us: keys_values_of(): head_unit(mixed[..., :model_width]).astype(jnp.bfloat16)]
    reduce_sum x7 -> x0, other arithmetic: 6.5 us -> none  [the longest x2 4.55 us: head_unit(): energy = jnp.mean(shaped * shaped, axis=-1, keepdims=True)]
  transfers between devices with their start and end apart: 12 -> 0, of which waited for: 5 -> 0; matrix products, arithmetic and copies ran while one was open for 18% -> 0% of each run, Pallas kernels for 0% -> 0%
where the time goes in v1:
time: 35.2 us; the launch traced here: 35 us
  Pallas kernels  29.9 us (85%)
  local copies, waits for them, and re-layouts  5.04 us (14%)
    pallas_call x1, Pallas kernels, per_device(): pl.pallas_call(functools.partial(scene_kernel, n), out_shape=jax.ShapeDty...  29.9 us
    pallas_call x1, local copies, waits for them, and re-layouts, per_device(): pl.pallas_call(functools.partial(scene_kernel, n), out_shape=jax.ShapeDty...  2.51 us
    broadcast_in_dim x1, local copies, waits for them, and re-layouts, per_device(): head_gain[None]  1.27 us
    broadcast_in_dim x1, local copies, waits for them, and re-layouts, per_device(): attn_gain[None]  1.27 us

profile of v1, /device:TPU:0, one launch (start us, length us, event | category | flops | bytes accessed | tf_op | source)
XLA Modules:
  0.0 35.0 jit_solution(6585519890596571285)
XLA Ops:
  0.0 1.3 %broadcast_in_dim.9.attn_gain_ref = f32[1,768]{1,0:T(1,128)} reshape(f32[768]{0:T(1024)} %param.12) | data formatting | bytes 6144 | tf_op jit(solution)/shard_map/broadcast_in_dim | solution.py:238
  1.3 1.3 %broadcast_in_dim.10.head_gain_ref = f32[1,768]{1,0:T(1,128)} reshape(f32[768]{0:T(1024)} %param.13) | data formatting | bytes 6144 | tf_op jit(solution)/shard_map/broadcast_in_dim | solution.py:239
  2.5 29.9 %scene.1 = f32[1,196,768]{2,1,0:T(8,128)} custom-call(bf16[1,196,768]{2,1,0:T(8,128)(2,1)} %tokens_ref.1, f32[1,768]{1,0:T(1,128)} %broadcast_in_dim.9.attn_gain_ref, f32[1,768]{1,0:T(1,128)} %broadcast_in_dim.10.head_gain_ref, f32[1,1024]{1,0:T(1,128)} %bitcast.2, s32[2,32]{1,0:T(2,128)} %bitcast.3, s32[16]{0:T(128)} %count_ref.1, ...), custom_call_target="tpu_custom_call" | custom-call | tf_op jit(solution)/shard_map/scene/pallas_call | solution.py:212
  32.5 2.5 %copy.10 = f32[1,196,768]{2,0,1:T(1,128)} copy(f32[1,196,768]{2,1,0:T(8,128)} %scene.1) | data formatting | bytes 1204224 | tf_op jit(solution)/shard_map/scene/pallas_call | solution.py:212

commit v2 on v1

--- a/solution.py
+++ b/solution.py
@@ -19,7 +19,7 @@
 def layer_norm(values, gain_row):
     centred = values - jnp.mean(values, axis=-1, keepdims=True)
     spread = jnp.mean(centred * centred, axis=-1, keepdims=True)
-    return centred * lax.rsqrt(spread + EPSILON) * gain_row
+    return centred * lax.rsqrt(spread + EPSILON) * gain_row[None]
 
 
 def product(left, right):
@@ -95,9 +95,8 @@
         return copy
 
     copies = {}
+    copies[MATE] = send(own_ref, MATE, 1)
     copies[AHEAD] = send(own_ref, AHEAD, -2)
-    copies[BEHIND] = send(own_ref, BEHIND, 2)
-    copies[MATE] = send(own_ref, MATE, 1)
 
     across = lax.broadcasted_iota(jnp.int32, (group, group), 0) // head
     along = lax.broadcasted_iota(jnp.int32, (group, group), 1) // head
@@ -176,18 +175,20 @@
 
     copies[MATE].wait_recv()
     view(MATE, 1, True)
+    copies[AHEAD].wait_send()
+    copies[BEHIND] = send(own_ref, BEHIND, 2)
     copies[AHEAD].wait_recv()
     copies[RELAYED] = send(recv_ref.at[AHEAD], RELAYED, 1)
     view(AHEAD, 2, False)
+    copies[RELAYED].wait_recv()
+    view(RELAYED, -1, False)
     copies[BEHIND].wait_recv()
     view(BEHIND, -2, False)
-    copies[RELAYED].wait_recv()
-    view(RELAYED, -1, False)
 
     for c in range(3):
         cols = slice(c * pixels, (c + 1) * pixels)
         joined_ref[0, :, cols] = (sum_ref[:, cols] / weight_ref[...])[:token_count]
-    for slot in range(4):
+    for slot in (MATE, BEHIND, RELAYED):
         copies[slot].wait_send()
 
 
@@ -235,8 +236,8 @@
         name="scene",
     )(
         tokens,
-        attn_gain[None],
-        head_gain[None],
+        attn_gain,
+        head_gain,
         head_bias[None],
         pair_list.T,
         pair_count,

time: 35.2 us -> 28.9 us (0.82)
  Pallas kernels: 29.9 us -> 26.2 us
  local copies, waits for them, and re-layouts: 5.04 us -> 2.51 us
    pallas_call x1, Pallas kernels: 29.9 us -> 26.2 us  [per_device(): pl.pallas_call(functools.partial(scene_kernel, n), out_shape=jax.ShapeDty...]
    broadcast_in_dim x2 -> x0, local copies, waits for them, and re-layouts: 2.53 us -> none  [the longest x1 1.27 us: per_device(): head_gain[None]]
where the time goes in v2:
time: 28.9 us; the launch traced here: 28.7 us
  Pallas kernels  26.2 us (91%)
  local copies, waits for them, and re-layouts  2.51 us (9%)
    pallas_call x1, Pallas kernels, per_device(): pl.pallas_call(functools.partial(scene_kernel, n), out_shape=jax.ShapeDty...  26.2 us
    pallas_call x1, local copies, waits for them, and re-layouts, per_device(): pl.pallas_call(functools.partial(scene_kernel, n), out_shape=jax.ShapeDty...  2.51 us

profile of v2, /device:TPU:0, one launch (start us, length us, event | category | flops | bytes accessed | tf_op | source)
XLA Modules:
  0.0 28.7 jit_solution(7327821101577893019)
XLA Ops:
  0.0 26.2 %scene.1 = f32[1,196,768]{2,1,0:T(8,128)} custom-call(bf16[1,196,768]{2,1,0:T(8,128)(2,1)} %tokens_ref.1, f32[768]{0:T(1024)} %attn_gain_ref.1, f32[768]{0:T(1024)} %head_gain_ref.1, f32[1,1024]{1,0:T(1,128)} %bitcast.2, s32[2,32]{1,0:T(2,128)} %bitcast.3, s32[16]{0:T(128)} %count_ref.1, bf16[768,2304]{1,0:T(8,128)(2,1)} %qkv_hbm.1, ...), custom_call_target="tpu_custom_call" | custom-call | tf_op jit(solution)/shard_map/scene/pallas_call | solution.py:213
  26.2 2.5 %copy.10 = f32[1,196,768]{2,0,1:T(1,128)} copy(f32[1,196,768]{2,1,0:T(8,128)} %scene.1) | data formatting | bytes 1204224 | tf_op jit(solution)/shard_map/scene/pallas_call | solution.py:213

commit v3 on v2

--- a/solution.py
+++ b/solution.py
@@ -75,8 +75,7 @@
     barrier = pltpu.get_barrier_semaphore()
     for steps in (1, 2, -2):
         pl.semaphore_signal(barrier, inc=1, device_id={"scene": at(steps)})
-    for load in loads:
-        load.start()
+    loads[0].start()
 
     rows_ref[...] = jnp.zeros_like(rows_ref)
     rows_ref[0:token_count] = tokens_ref[0].astype(F32)
@@ -95,8 +94,10 @@
         return copy
 
     copies = {}
+    copies[AHEAD] = send(own_ref, AHEAD, -2)
     copies[MATE] = send(own_ref, MATE, 1)
-    copies[AHEAD] = send(own_ref, AHEAD, -2)
+    for load in loads[1:]:
+        load.start()
 
     across = lax.broadcasted_iota(jnp.int32, (group, group), 0) // head
     along = lax.broadcasted_iota(jnp.int32, (group, group), 1) // head

time: 28.9 us -> 28.9 us (level)
  no operation moved by 1% of the time
where the time goes in v3:
time: 28.9 us; the launch traced here: 28.7 us
  Pallas kernels  26.2 us (91%)
  local copies, waits for them, and re-layouts  2.51 us (9%)
    pallas_call x1, Pallas kernels, per_device(): pl.pallas_call(functools.partial(scene_kernel, n), out_shape=jax.ShapeDty...  26.2 us
    pallas_call x1, local copies, waits for them, and re-layouts, per_device(): pl.pallas_call(functools.partial(scene_kernel, n), out_shape=jax.ShapeDty...  2.51 us

profile of v3, /device:TPU:0, one launch (start us, length us, event | category | flops | bytes accessed | tf_op | source)
XLA Modules:
  0.0 28.7 jit_solution(9932357938951289201)
XLA Ops:
  0.0 26.2 %scene.1 = f32[1,196,768]{2,1,0:T(8,128)} custom-call(bf16[1,196,768]{2,1,0:T(8,128)(2,1)} %tokens_ref.1, f32[768]{0:T(1024)} %attn_gain_ref.1, f32[768]{0:T(1024)} %head_gain_ref.1, f32[1,1024]{1,0:T(1,128)} %bitcast.2, s32[2,32]{1,0:T(2,128)} %bitcast.3, s32[16]{0:T(128)} %count_ref.1, bf16[768,2304]{1,0:T(8,128)(2,1)} %qkv_hbm.1, ...), custom_call_target="tpu_custom_call" | custom-call | tf_op jit(solution)/shard_map/scene/pallas_call | solution.py:214
  26.2 2.5 %copy.10 = f32[1,196,768]{2,0,1:T(1,128)} copy(f32[1,196,768]{2,1,0:T(8,128)} %scene.1) | data formatting | bytes 1204224 | tf_op jit(solution)/shard_map/scene/pallas_call | solution.py:214
